TPU v7x, 32 devices: a whole 2x2x4 slice. The times are simulated.
32 devices in a mesh: grp: 4 (over y, core), dev: 8 (over z, x).
Axes of the slice: x: 2, y: 2, z: 4, core: 2. Of those that a mesh axis runs over, the one named last changes fastest.
Arguments:
- tiles: bfloat16 [4, 8192, 4096], P('grp', 'dev'), may hold values from -0.75 to 0.75
- owner: int32 [4, 8192, 1], P('grp', 'dev'), may hold values from 0 to 7; in each aligned block of 1024 rows (0 to 1023, 1024 to 2047, ..., all dimensions but the last counted through in order) at most 256 rows name the same one
- target: int32 [4, 8192], P('grp', 'dev'), may hold values from 0 to 159
- mass: float32 [4, 16384], P('grp', 'dev'), may hold values from 30 to 100
- rhs: float32 [4, 16384], P('grp', 'dev'), may hold values from -1200 to 1200
- faces: int32 [4, 4, 256], P(None, 'grp', 'dev'), may hold values from 0 to 31, as said below
Outputs:
- smoothed: float32 [4, 16384], P('grp', 'dev')
Inputs may be any that keep to these rules, and one draw needn't show every extreme that they name: At most 256 tiles of one device have the same owner. `faces`: each entry names a row block of another colour than its own row block.
All inputs are finite; a program needn't handle non-finite values.
Results may differ from a plain program's by a relative error of at most 0.0003.
Values may be sent and summed in bfloat16 or wider, within the bound.
A program may use at most 128 MiB of HBM per device.

v0:
```python
import jax
import jax.numpy as jnp
from jax import lax
from jax.sharding import PartitionSpec as P

BLK = 64
COLOURS = 4
SWEEPS = 2


def padded(array, sides, width):
    for axis, dim in sides:
        peers, length = (lax.axis_size(axis), array.shape[dim])
        up = [(i, (i + 1) % peers) for i in range(peers - 1)]
        down = [(j, i) for i, j in up]
        last = lax.slice_in_dim(array, length - width, length, axis=dim)
        leading = lax.slice_in_dim(array, 0, width, axis=dim)
        before = lax.ppermute(last, axis, up)
        after = lax.ppermute(leading, axis, down)
        array = jnp.concatenate([before, array, after], axis=dim)
    return array


def share(fresh):
    grid = padded(fresh.reshape(1, 1, -1), (("grp", 0), ("dev", 1)), 1)
    return jnp.stack([grid[1, 0], grid[1, 2], grid[0, 1], grid[2, 1]]).reshape(
        4, fresh.shape[0], fresh.shape[1]
    )


def pack_slots(tiles_dev, aim, where_to, peers, slots, keep):
    width = tiles_dev.shape[1]
    place = jnp.where(keep, where_to, peers * slots)
    packed = jnp.zeros((peers * slots, width), jnp.bfloat16).at[place].set(tiles_dev, mode="drop")
    labels = jnp.full((peers * slots,), -1, jnp.int32).at[place].set(aim, mode="drop")
    return (packed.reshape(peers, slots, width), labels.reshape(peers, slots))


def add_tiles(got, got_labels, slots_dev):
    width = got.shape[2]
    picks = (got_labels.reshape(1, -1) == lax.iota(jnp.int32, slots_dev)[:, None]).astype(
        jnp.bfloat16
    )
    return jnp.dot(picks, got.reshape(-1, width), preferred_element_type=jnp.float32)


def body(tiles, owner, target, mass, rhs, faces):
    count = tiles.shape[1]
    rowblk = mass.shape[1] // BLK
    colblk = rowblk // COLOURS
    peers = lax.axis_size("dev")
    slots_dev = rowblk * 5
    dest = owner[0, :, 0]
    aim = target[0]
    cap = max(2, 2 * count // peers)
    member = (dest[:, None] == lax.iota(jnp.int32, peers)[None, :]).astype(jnp.int32)
    order = jnp.sum((jnp.cumsum(member, axis=0) - 1) * member, axis=1)
    packed, labels = pack_slots(tiles[0], aim, dest * cap + order, peers, cap, order >= 0)
    got, got_labels = (
        lax.all_to_all(packed, "dev", split_axis=0, concat_axis=0, tiled=True),
        lax.all_to_all(labels, "dev", split_axis=0, concat_axis=0, tiled=True),
    )
    assembled = add_tiles(got, got_labels, slots_dev)
    blocks = assembled.reshape(rowblk, 5, BLK, BLK)
    scale = mass.reshape(rowblk, BLK)
    load = rhs.reshape(rowblk, BLK)
    links = faces[:, 0, :]
    denom = scale + jnp.sum(jnp.abs(blocks), axis=(1, 3))
    state = jnp.zeros((rowblk, BLK), jnp.float32)
    nearby = jnp.zeros((4, rowblk, BLK), jnp.float32)
    high = lax.Precision.HIGHEST
    for sweep in range(SWEEPS):
        for colour in range(COLOURS):
            low = colour * colblk
            upper = low + colblk
            seen = jnp.stack(
                [jnp.take(nearby[face], links[face, low:upper], axis=0) for face in range(4)],
                axis=1,
            )
            own = state[low:upper]
            applied = jnp.einsum("rij,rj->ri", blocks[low:upper, 0], own, precision=high)
            applied = applied + jnp.einsum(
                "rfij,rfj->ri", blocks[low:upper, 1:], seen, precision=high
            )
            resid = load[low:upper] - scale[low:upper] * own - applied
            state = state.at[low:upper].set(own + resid / denom[low:upper])
            if sweep + 1 < SWEEPS or colour + 1 < COLOURS:
                nearby = nearby.at[:, low:upper].set(share(state[low:upper]))
    return state.reshape(1, -1)


def solution(mesh):
    placed = (
        P("grp", "dev", None),
        P("grp", "dev", None),
        P("grp", "dev"),
        P("grp", "dev"),
        P("grp", "dev"),
        P(None, "grp", "dev"),
    )
    return jax.shard_map(
        body, mesh=mesh, in_specs=placed, out_specs=P("grp", "dev"), check_vma=False
    )
```

profile of v0, /device:TPU:0, one launch (start us, length us, event | category | flops | bytes accessed | tf_op | source)
XLA Modules:
  0.0 646.5 jit_solution(10107362470813299100)
XLA Ops:
  0.7 2.3 reduce-window.6
  4.9 22.0 %scatter_custom_fusion.1 = bf16[2048,4096]{1,0:T(8,128)(2,1)} fusion(s32[1024]{0:T(1024)S(1)} %bitcast.336, bf16[1,1024,4096]{2,1,0:T(8,128)(2,1)} %param.38, bf16[]{:T(256)} %constant.383.clone.1), kind=kCustom, calls=%fused_computation.34 | custom fusion | bytes 25165826 | tf_op jit(solution)/shard_map/scatter | solution.py:34
  26.9 7.4 %all-to-all-start.1 = ((bf16[8,256,4096]{2,1,0:T(8,128)(2,1)}), bf16[8,256,4096]{2,1,0:T(8,128)(2,1)}, u32[]{:S(2)}, u32[]{:S(2)}) async-start(bf16[8,256,4096]{2,1,0:T(8,128)(2,1)} %bitcast.304), calls=%async_computation.1 | async-start | bytes 33554432 | tf_op jit(solution)/shard_map/all_to_all | solution.py:60
  37.4 5.0 scatter_custom_fusion
  45.2 352.2 %all-to-all-done.1 = bf16[8,256,4096]{2,1,0:T(8,128)(2,1)} async-done(((bf16[8,256,4096]{2,1,0:T(8,128)(2,1)}), bf16[8,256,4096]{2,1,0:T(8,128)(2,1)}, u32[]{:S(2)}, u32[]{:S(2)}) %all-to-all-start.1) | async-done | bytes 16777248 | tf_op jit(solution)/shard_map/all_to_all | solution.py:60
  397.4 3.5 all-to-all-start
  402.4 22.6 %copy.77 = bf16[2048,4096]{0,1:T(8,128)(2,1)} copy(bf16[2048,4096]{1,0:T(8,128)(2,1)} %bitcast.13) | data formatting | bytes 33554432 | tf_op jit(solution)/shard_map/reshape | solution.py:44
  425.0 11.2 %abs_reduce_fusion = (f32[32,64]{0,1:T(8,128)S(1)}, f32[32,5,64,64]{3,0,2,1:T(8,128)S(1)}) fusion(bf16[64,64,2048,1]{2,1,0,3:T(8,128)(2,1)} %bitcast.305, s32[32,5]{0,1:T(8,128)S(1)} %multiply_add_fusion, s32[2048]{0:T(1024)S(1)} %bitcast.335), kind=kOutput, calls=%fused_computation.37 | convolution fusion | flops 2685990912 | bytes 19415680 | tf_op jit(solution)/shard_map/dot_general | solution.py:44
  437.1 1.4 fusion.53
  438.6 1.5 fusion.38
  440.1 2.3 fusion.20
  442.6 1.6 collective-permute-start
  446.1 1.3 collective-permute-start.1
  448.1 2.5 collective-permute-done.1
  451.2 1.3 collective-permute-start.3
  452.5 2.1 fusion.34
  454.6 4.8 collective-permute-start.2
  461.2 2.0 gather_fusion.7
  463.2 1.3 select_bitcast_fusion.24
  471.9 3.4 collective-permute-start.4
  476.6 1.3 slice.650
  477.9 1.3 slice.652
  481.2 1.5 collective-permute-done.5
  483.3 1.3 collective-permute-start.7
  484.6 2.1 fusion.30
  486.7 5.4 collective-permute-start.6
  494.2 2.0 gather_fusion.11
  496.1 1.3 select_bitcast_fusion.20
  504.8 3.4 collective-permute-start.8
  509.5 1.3 slice.668
  510.8 1.3 slice.670
  514.0 1.5 collective-permute-done.9
  516.1 1.3 collective-permute-start.11
  518.6 5.7 collective-permute-start.10
  526.3 2.0 gather_fusion.15
  528.3 1.3 select_bitcast_fusion.16
  537.1 3.4 collective-permute-start.12
  540.5 1.3 collective-permute-start.13
  542.4 1.5 collective-permute-done.13
  544.6 1.3 collective-permute-start.15
  545.9 2.1 fusion.36
  547.9 5.7 collective-permute-start.14
  555.7 2.0 gather_fusion.19
  557.7 1.4 select_bitcast_fusion.12
  564.5 2.3 fusion.18
  567.7 3.4 collective-permute-start.16
  571.1 1.3 collective-permute-start.17
  573.0 1.5 collective-permute-done.17
  575.2 1.3 collective-permute-start.19
  576.5 2.1 fusion.32
  578.5 5.7 collective-permute-start.18
  586.3 2.0 gather_fusion.23
  588.3 1.3 select_bitcast_fusion.8
  597.0 3.4 collective-permute-start.20
  600.4 1.3 collective-permute-start.21
  602.4 1.5 collective-permute-done.21
  604.5 1.3 collective-permute-start.23
  605.8 1.5 fusion.28
  607.3 5.7 collective-permute-start.22
  621.8 3.4 collective-permute-start.24
  625.2 1.3 collective-permute-start.25
  627.1 1.5 collective-permute-done.25
  629.3 1.3 collective-permute-start.27
  631.1 5.7 collective-permute-start.26
  (249 shorter events, 92.8 us)
Async XLA Ops:
  26.9 7.4 %copy-start.2 = (s32[4,1,32]{2,1,0:T(1,128)S(1)}, s32[4,1,32]{2,1,0:T(1,128)}, u32[]{:S(2)}) copy-start(s32[4,1,32]{2,1,0:T(1,128)} %param.43) | copy-start | bytes 1540
  26.9 17.7 %copy-start.3 = (f32[1,2048]{1,0:T(1,128)S(1)}, f32[1,2048]{1,0:T(1,128)}, u32[]{:S(2)}) copy-start(f32[1,2048]{1,0:T(1,128)} %param.41) | copy-start | bytes 24580
  26.9 17.7 %copy-start.4 = (f32[1,2048]{1,0:T(1,128)S(1)}, f32[1,2048]{1,0:T(1,128)}, u32[]{:S(2)}) copy-start(f32[1,2048]{1,0:T(1,128)} %param.42) | copy-start | bytes 24580
  26.9 370.5 %all-to-all-start.1 = ((bf16[8,256,4096]{2,1,0:T(8,128)(2,1)}), bf16[8,256,4096]{2,1,0:T(8,128)(2,1)}, u32[]{:S(2)}, u32[]{:S(2)}) async-start(bf16[8,256,4096]{2,1,0:T(8,128)(2,1)} %bitcast.304), calls=%async_computation.1 | async-start | bytes 33554432 | tf_op jit(solution)/shard_map/all_to_all | solution.py:60
  35.0 389.9 %copy-start.9 = (pred[8]{0:T(512)(128)(4,1)}, pred[8]{0:T(512)(128)(4,1)S(1)}, u32[]{:S(2)}) copy-start(pred[8]{0:T(512)(128)(4,1)S(1)} %get-tuple-element.318) | copy-start | bytes 28
  35.0 389.9 %copy-start.10 = (pred[8]{0:T(512)(128)(4,1)}, pred[8]{0:T(512)(128)(4,1)S(1)}, u32[]{:S(2)}) copy-start(pred[8]{0:T(512)(128)(4,1)S(1)} %get-tuple-element.316) | copy-start | bytes 28
  35.0 389.9 %copy-start.11 = (pred[8]{0:T(512)(128)(4,1)}, pred[8]{0:T(512)(128)(4,1)S(1)}, u32[]{:S(2)}) copy-start(pred[8]{0:T(512)(128)(4,1)S(1)} %get-tuple-element.314) | copy-start | bytes 28
  35.0 389.9 %copy-start.12 = (pred[8]{0:T(512)(128)(4,1)}, pred[8]{0:T(512)(128)(4,1)S(1)}, u32[]{:S(2)}) copy-start(pred[8]{0:T(512)(128)(4,1)S(1)} %get-tuple-element.312) | copy-start | bytes 28
  35.0 0.6 copy-start.8
  35.1 1.2 copy-start.6
  36.2 0.6 copy-start.7
  36.2 388.7 %copy-start.5 = (s32[1024]{0:T(1024)}, s32[1024]{0:T(1024)S(1)}, u32[]{:S(2)}) copy-start(s32[1024]{0:T(1024)S(1)} %get-tuple-element.349) | copy-start | bytes 12292
  397.4 27.6 %all-to-all-start = ((s32[8,1,256]{2,1,0:T(1,128)}), s32[8,1,256]{2,1,0:T(1,128)S(1)}, u32[]{:S(2)}, u32[]{:S(2)}) async-start(s32[8,1,256]{2,1,0:T(1,128)} %bitcast.7), calls=%async_computation | async-start | bytes 16384 | tf_op jit(solution)/shard_map/all_to_all | solution.py:61
  401.0 41.5 %copy-start = (f32[8,64]{1,0:T(8,128)}, f32[8,64]{1,0:T(8,128)S(1)}, u32[]{:S(2)}) copy-start(f32[8,64]{1,0:T(8,128)S(1)} %slice.618) | copy-start | bytes 6148
  401.1 41.4 %copy-start.1 = (f32[8,64]{1,0:T(8,128)}, f32[8,64]{1,0:T(8,128)S(1)}, u32[]{:S(2)}) copy-start(f32[8,64]{1,0:T(8,128)S(1)} %slice.620) | copy-start | bytes 6148
  442.6 4.8 collective-permute-start
  446.1 4.5 collective-permute-start.1
  451.2 8.3 %collective-permute-start.3 = (f32[3,1,512]{2,1,0:T(1,128)S(1)}, f32[3,1,512]{2,1,0:T(1,128)S(1)}, u32[]{:S(2)}, u32[]{:S(2)}) collective-permute-start(f32[3,1,512]{2,1,0:T(1,128)S(1)} %get-tuple-element.328), channel_id=1, source_target_pairs={{1,0},{2,1},{3,2},{4,3},{5,4},{6,5},{7,6},{9,8},{10,9},{11,10},{12... | collective-permute-start | bytes 18440 | tf_op jit(solution)/shard_map/ppermute | solution.py:19
  454.6 5.9 collective-permute-start.2
  471.9 8.6 %collective-permute-start.4 = (f32[1,1,512]{2,1,0:T(1,128)S(1)}, f32[1,1,512]{2,1,0:T(1,128)S(1)}, u32[]{:S(2)}, u32[]{:S(2)}) collective-permute-start(f32[1,1,512]{2,1,0:T(1,128)S(1)} %reshape.580), channel_id=1, source_target_pairs={{0,8},{8,16},{16,24},{1,9},{9,17},{17,25},{2,10},{10,18},{18,26},{... | collective-permute-start | bytes 6152 | tf_op jit(solution)/shard_map/ppermute | solution.py:18
  479.2 3.4 collective-permute-start.5
  483.3 9.0 %collective-permute-start.7 = (f32[3,1,512]{2,1,0:T(1,128)S(1)}, f32[3,1,512]{2,1,0:T(1,128)S(1)}, u32[]{:S(2)}, u32[]{:S(2)}) collective-permute-start(f32[3,1,512]{2,1,0:T(1,128)S(1)} %get-tuple-element.324), channel_id=1, source_target_pairs={{1,0},{2,1},{3,2},{4,3},{5,4},{6,5},{7,6},{9,8},{10,9},{11,10},{12... | collective-permute-start | bytes 18440 | tf_op jit(solution)/shard_map/ppermute | solution.py:19
  486.7 6.8 %collective-permute-start.6 = (f32[3,1,512]{2,1,0:T(1,128)S(1)}, f32[3,1,512]{2,1,0:T(1,128)S(1)}, u32[]{:S(2)}, u32[]{:S(2)}) collective-permute-start(f32[3,1,512]{2,1,0:T(1,128)S(1)} %get-tuple-element.324), channel_id=1, source_target_pairs={{0,1},{1,2},{2,3},{3,4},{4,5},{5,6},{6,7},{8,9},{9,10},{10,11},{11... | collective-permute-start | bytes 18440 | tf_op jit(solution)/shard_map/ppermute | solution.py:18
  504.8 8.6 %collective-permute-start.8 = (f32[1,1,512]{2,1,0:T(1,128)S(1)}, f32[1,1,512]{2,1,0:T(1,128)S(1)}, u32[]{:S(2)}, u32[]{:S(2)}) collective-permute-start(f32[1,1,512]{2,1,0:T(1,128)S(1)} %reshape.581), channel_id=1, source_target_pairs={{0,8},{8,16},{16,24},{1,9},{9,17},{17,25},{2,10},{10,18},{18,26},{... | collective-permute-start | bytes 6152 | tf_op jit(solution)/shard_map/ppermute | solution.py:18
  512.0 3.4 collective-permute-start.9
  516.1 8.3 %collective-permute-start.11 = (f32[3,1,512]{2,1,0:T(1,128)S(1)}, f32[3,1,512]{2,1,0:T(1,128)S(1)}, u32[]{:S(2)}, u32[]{:S(2)}) collective-permute-start(f32[3,1,512]{2,1,0:T(1,128)S(1)} %get-tuple-element.320), channel_id=1, source_target_pairs={{1,0},{2,1},{3,2},{4,3},{5,4},{6,5},{7,6},{9,8},{10,9},{11,10},{12... | collective-permute-start | bytes 18440 | tf_op jit(solution)/shard_map/ppermute | solution.py:19
  518.6 7.0 %collective-permute-start.10 = (f32[3,1,512]{2,1,0:T(1,128)S(1)}, f32[3,1,512]{2,1,0:T(1,128)S(1)}, u32[]{:S(2)}, u32[]{:S(2)}) collective-permute-start(f32[3,1,512]{2,1,0:T(1,128)S(1)} %get-tuple-element.320), channel_id=1, source_target_pairs={{0,1},{1,2},{2,3},{3,4},{4,5},{5,6},{6,7},{8,9},{9,10},{10,11},{11... | collective-permute-start | bytes 18440 | tf_op jit(solution)/shard_map/ppermute | solution.py:18
  537.1 4.7 collective-permute-start.12
  540.5 3.5 collective-permute-start.13
  544.6 9.2 %collective-permute-start.15 = (f32[3,1,512]{2,1,0:T(1,128)S(1)}, f32[3,1,512]{2,1,0:T(1,128)S(1)}, u32[]{:S(2)}, u32[]{:S(2)}) collective-permute-start(f32[3,1,512]{2,1,0:T(1,128)S(1)} %get-tuple-element.286), channel_id=1, source_target_pairs={{1,0},{2,1},{3,2},{4,3},{5,4},{6,5},{7,6},{9,8},{10,9},{11,10},{12... | collective-permute-start | bytes 18440 | tf_op jit(solution)/shard_map/ppermute | solution.py:19
  547.9 7.0 %collective-permute-start.14 = (f32[3,1,512]{2,1,0:T(1,128)S(1)}, f32[3,1,512]{2,1,0:T(1,128)S(1)}, u32[]{:S(2)}, u32[]{:S(2)}) collective-permute-start(f32[3,1,512]{2,1,0:T(1,128)S(1)} %get-tuple-element.286), channel_id=1, source_target_pairs={{0,1},{1,2},{2,3},{3,4},{4,5},{5,6},{6,7},{8,9},{9,10},{10,11},{11... | collective-permute-start | bytes 18440 | tf_op jit(solution)/shard_map/ppermute | solution.py:18
  567.7 4.7 collective-permute-start.16
  571.1 3.5 collective-permute-start.17
  575.2 9.2 %collective-permute-start.19 = (f32[3,1,512]{2,1,0:T(1,128)S(1)}, f32[3,1,512]{2,1,0:T(1,128)S(1)}, u32[]{:S(2)}, u32[]{:S(2)}) collective-permute-start(f32[3,1,512]{2,1,0:T(1,128)S(1)} %get-tuple-element.282), channel_id=1, source_target_pairs={{1,0},{2,1},{3,2},{4,3},{5,4},{6,5},{7,6},{9,8},{10,9},{11,10},{12... | collective-permute-start | bytes 18440 | tf_op jit(solution)/shard_map/ppermute | solution.py:19
  578.5 7.0 %collective-permute-start.18 = (f32[3,1,512]{2,1,0:T(1,128)S(1)}, f32[3,1,512]{2,1,0:T(1,128)S(1)}, u32[]{:S(2)}, u32[]{:S(2)}) collective-permute-start(f32[3,1,512]{2,1,0:T(1,128)S(1)} %get-tuple-element.282), channel_id=1, source_target_pairs={{0,1},{1,2},{2,3},{3,4},{4,5},{5,6},{6,7},{8,9},{9,10},{10,11},{11... | collective-permute-start | bytes 18440 | tf_op jit(solution)/shard_map/ppermute | solution.py:18
  597.0 4.7 collective-permute-start.20
  600.4 3.5 collective-permute-start.21
  604.5 8.7 %collective-permute-start.23 = (f32[3,1,512]{2,1,0:T(1,128)S(1)}, f32[3,1,512]{2,1,0:T(1,128)S(1)}, u32[]{:S(2)}, u32[]{:S(2)}) collective-permute-start(f32[3,1,512]{2,1,0:T(1,128)S(1)} %get-tuple-element.278), channel_id=1, source_target_pairs={{1,0},{2,1},{3,2},{4,3},{5,4},{6,5},{7,6},{9,8},{10,9},{11,10},{12... | collective-permute-start | bytes 18440 | tf_op jit(solution)/shard_map/ppermute | solution.py:19
  607.3 7.1 %collective-permute-start.22 = (f32[3,1,512]{2,1,0:T(1,128)S(1)}, f32[3,1,512]{2,1,0:T(1,128)S(1)}, u32[]{:S(2)}, u32[]{:S(2)}) collective-permute-start(f32[3,1,512]{2,1,0:T(1,128)S(1)} %get-tuple-element.278), channel_id=1, source_target_pairs={{0,1},{1,2},{2,3},{3,4},{4,5},{5,6},{6,7},{8,9},{9,10},{10,11},{11... | collective-permute-start | bytes 18440 | tf_op jit(solution)/shard_map/ppermute | solution.py:18
  621.8 4.7 collective-permute-start.24
  625.2 3.5 collective-permute-start.25
  629.3 7.7 %collective-permute-start.27 = (f32[3,1,512]{2,1,0:T(1,128)S(1)}, f32[3,1,512]{2,1,0:T(1,128)S(1)}, u32[]{:S(2)}, u32[]{:S(2)}) collective-permute-start(f32[3,1,512]{2,1,0:T(1,128)S(1)} %get-tuple-element.274), channel_id=1, source_target_pairs={{1,0},{2,1},{3,2},{4,3},{5,4},{6,5},{7,6},{9,8},{10,9},{11,10},{12... | collective-permute-start | bytes 18440 | tf_op jit(solution)/shard_map/ppermute | solution.py:19
  631.1 7.1 %collective-permute-start.26 = (f32[3,1,512]{2,1,0:T(1,128)S(1)}, f32[3,1,512]{2,1,0:T(1,128)S(1)}, u32[]{:S(2)}, u32[]{:S(2)}) collective-permute-start(f32[3,1,512]{2,1,0:T(1,128)S(1)} %get-tuple-element.274), channel_id=1, source_target_pairs={{0,1},{1,2},{2,3},{3,4},{4,5},{5,6},{6,7},{8,9},{9,10},{10,11},{11... | collective-permute-start | bytes 18440 | tf_op jit(solution)/shard_map/ppermute | solution.py:18
where the time goes:
time: 655 us; the launch traced here: 646 us
  waiting for transfers between devices  371 us (57%)
  local copies, waits for them, and re-layouts  107 us (16%)
  starting transfers between devices  89.7 us (14%)
  other arithmetic  43 us (7%)
  matrix products  35.5 us (5%)
    all_to_all x1, waiting for transfers between devices, body(): lax.all_to_all(packed, 'dev', split_axis=0, concat_axis=0, tiled=True)  352 us
    ppermute x14, starting transfers between devices, padded(): before = lax.ppermute(last, axis, up)  60.7 us
    gather x32, local copies, waits for them, and re-layouts, body(): jnp.take(nearby[face], links[face, low:upper], axis=0)  30.6 us
    another operation x40, other arithmetic, body(): jnp.stack([jnp.take(nearby[face], links[face, low:upper], axis=0) for fac...  27 us
    reshape x1, local copies, waits for them, and re-layouts, add_tiles(): got.reshape(-1, width)  22.6 us
    scatter x1, local copies, waits for them, and re-layouts, pack_slots(): jnp.zeros((peers * slots, width), jnp.bfloat16).at[place]  22 us
    ppermute x14, starting transfers between devices, padded(): after = lax.ppermute(leading, axis, down)  18 us
  transfers between devices with their start and end apart: 30, of which 15 were waited for; matrix products, arithmetic and copies ran while one was open for 10% of the time, Pallas kernels for 0%

commit v1 on v0

--- a/solution.py
+++ b/solution.py
@@ -1,11 +1,16 @@
+import functools
+
 import jax
 import jax.numpy as jnp
 from jax import lax
+from jax.experimental import pallas as pl
+from jax.experimental.pallas import tpu as pltpu
 from jax.sharding import PartitionSpec as P
 
 BLK = 64
 COLOURS = 4
 SWEEPS = 2
+MESH = pl.DeviceIdType.MESH
 
 
 def padded(array, sides, width):
@@ -88,6 +93,297 @@
                 nearby = nearby.at[:, low:upper].set(share(state[low:upper]))
     return state.reshape(1, -1)
 
+def assemble_and_smooth(pairs, cols, names, tiles_hbm, key_ref, right_ref, mass_ref, load_ref, faces_ref, out_ref,
+                        tiles_v, pick_far, pick_own, far_send, far_recv, acc, line_send, up_recv, down_recv,
+                        spread, mat, norm, state, near, seen, prod, fresh, face_recv,
+                        tile_sem, far_ssem, far_rsem, line_ssem, up_rsem, down_rsem, fresh_ssem, face_rsem):
+    grp = lax.axis_index("grp")
+    dev = lax.axis_index("dev")
+    n_grp, n_dev = names
+    z = dev // 2
+    x = dev % 2
+    chunks = tiles_v.shape[0]
+    slots = mat.shape[1]
+    colblk = slots // (5 * COLOURS)
+    near_by = [
+        (dev >= 1, {"dev": dev - 1}),
+        (dev < n_dev - 1, {"dev": dev + 1}),
+        (grp >= 1, {"grp": grp - 1}),
+        (grp < n_grp - 1, {"grp": grp + 1}),
+    ]
+    partners = near_by + [(dev >= 2, {"dev": dev - 2}), (dev < n_dev - 2, {"dev": dev + 2})]
+
+    def load_tiles(k):
+        return pltpu.make_async_copy(
+            tiles_hbm.at[0, :, pl.ds(pl.multiple_of(k * cols, cols), cols)], tiles_v.at[k], tile_sem.at[k]
+        )
+
+    for k in range(chunks):
+        load_tiles(k).start()
+
+    barrier = pltpu.get_barrier_semaphore()
+    for there, who in partners:
+        @pl.when(there)
+        def _():
+            pl.semaphore_signal(barrier, inc=1, device_id=who, device_id_type=MESH)
+
+    key = key_ref[...]
+    right = right_ref[...]
+    key_far = jnp.where(right != x, key, -1)
+    key_own = jnp.where(right == x, key, -1)
+    rows = lax.broadcasted_iota(jnp.int32, (slots, key.shape[1]), 0)
+    for d in range(pairs):
+        part = slice(d * slots, (d + 1) * slots)
+        pick_far[part, :] = jnp.where(rows + d * slots == key_far, 1.0, 0.0).astype(jnp.bfloat16)
+
+    pl.semaphore_wait(barrier, sum(there.astype(jnp.int32) for there, who in partners))
+
+    def far_copy(k):
+        return pltpu.make_async_remote_copy(
+            src_ref=far_send.at[k], dst_ref=far_recv.at[k], send_sem=far_ssem.at[k], recv_sem=far_rsem.at[k],
+            device_id={"dev": z * 2 + 1 - x}, device_id_type=MESH,
+        )
+
+    def up_copy(k, d):
+        return pltpu.make_async_remote_copy(
+            src_ref=line_send.at[k, d], dst_ref=up_recv.at[k, d], send_sem=line_ssem.at[k, d],
+            recv_sem=up_rsem.at[k, d], device_id={"dev": dev + 2}, device_id_type=MESH,
+        )
+
+    def down_copy(k, d):
+        return pltpu.make_async_remote_copy(
+            src_ref=line_send.at[k, d], dst_ref=down_recv.at[k, d], send_sem=line_ssem.at[k, d],
+            recv_sem=down_rsem.at[k, d], device_id={"dev": dev - 2}, device_id_type=MESH,
+        )
+
+    def send_far(k, carry):
+        load_tiles(k).wait()
+        for d in range(pairs):
+            part = slice(d * slots, (d + 1) * slots)
+            far_send[k, part, :] = jnp.dot(
+                pick_far[part, :], tiles_v[k], preferred_element_type=jnp.float32
+            ).astype(jnp.bfloat16)
+        far_copy(k).start()
+        return carry
+
+    lax.fori_loop(0, chunks, send_far, 0)
+
+    for d in range(pairs):
+        part = slice(d * slots, (d + 1) * slots)
+        pick_own[part, :] = jnp.where(rows + d * slots == key_own, 1.0, 0.0).astype(jnp.bfloat16)
+    lane = lax.broadcasted_iota(jnp.int32, (cols, 128), 0) // BLK
+    unit = lax.broadcasted_iota(jnp.int32, (cols, 128), 1) % BLK
+    for k in range(chunks):
+        spread[k * cols:(k + 1) * cols, :] = jnp.where(lane + k * (cols // BLK) == unit, 1.0, 0.0).astype(jnp.bfloat16)
+    norm[...] = jnp.zeros_like(norm)
+    near[...] = jnp.zeros_like(near)
+    state[...] = jnp.zeros_like(state)
+
+    def split(value):
+        top = value.astype(jnp.bfloat16).astype(jnp.float32)
+        return jnp.concatenate([top, value - top], axis=0).astype(jnp.bfloat16)
+
+    def step(turn, carry):
+        @pl.when(turn < chunks)
+        def _():
+            k = turn
+            slot = lax.rem(k, 4)
+            far_copy(k).wait_recv()
+            for d in range(pairs):
+                part = slice(d * slots, (d + 1) * slots)
+                acc[slot, d] = jnp.dot(
+                    pick_own[part, :], tiles_v[k], preferred_element_type=jnp.float32
+                ) + far_recv[k, part, :].astype(jnp.float32)
+            for d in reversed(range(1, pairs)):
+                @pl.when(z == 0)
+                def _():
+                    line_send[k, d] = acc[slot, d].astype(jnp.bfloat16)
+                    up_copy(k, d).start()
+            for d in range(pairs - 1):
+                @pl.when(z == pairs - 1)
+                def _():
+                    line_send[k, d] = acc[slot, d].astype(jnp.bfloat16)
+                    down_copy(k, d).start()
+
+        @pl.when((turn >= 1) & (turn < chunks + 1))
+        def _():
+            k = turn - 1
+            slot = lax.rem(k, 4)
+            for e in range(1, pairs):
+                d = pairs - e
+                @pl.when((z > 0) & (z < d))
+                def _():
+                    up_copy(k, d).wait_recv()
+                    line_send[k, d] = (acc[slot, d] + up_recv[k, d].astype(jnp.float32)).astype(jnp.bfloat16)
+                    up_copy(k, d).start()
+                g = e - 1
+                @pl.when((z < pairs - 1) & (z > g))
+                def _():
+                    down_copy(k, g).wait_recv()
+                    line_send[k, g] = (acc[slot, g] + down_recv[k, g].astype(jnp.float32)).astype(jnp.bfloat16)
+                    down_copy(k, g).start()
+
+        @pl.when(turn >= 2)
+        def _():
+            k = turn - 2
+            slot = lax.rem(k, 4)
+            mat[k] = acc[slot, z]
+
+            @pl.when(z > 0)
+            def _():
+                up_copy(k, z).wait_recv()
+                mat[k] = mat[k] + up_recv[k, z].astype(jnp.float32)
+
+            @pl.when(z < pairs - 1)
+            def _():
+                down_copy(k, z).wait_recv()
+                mat[k] = mat[k] + down_recv[k, z].astype(jnp.float32)
+
+            size = jnp.abs(mat[k]).reshape(COLOURS, 5, colblk, cols)
+            size = jnp.sum(size, axis=1).reshape(COLOURS * colblk, cols)
+            norm[...] += jnp.dot(
+                split(size), spread[pl.ds(pl.multiple_of(k * cols, cols), cols), :],
+                preferred_element_type=jnp.float32,
+            )
+
+        return carry
+
+    lax.fori_loop(0, chunks + 2, step, 0)
+
+    half = COLOURS * colblk
+    norm[:half, :] = 1.0 / (mass_ref[...] + norm[:half, :] + norm[half:, :])
+
+    def fresh_copy(turn, face):
+        return pltpu.make_async_remote_copy(
+            src_ref=fresh.at[turn], dst_ref=face_recv.at[turn, face ^ 1], send_sem=fresh_ssem.at[turn, face],
+            recv_sem=face_rsem.at[turn, face ^ 1], device_id=near_by[face][1], device_id_type=MESH,
+        )
+
+    def face_wait(turn, face):
+        pltpu.make_async_remote_copy(
+            src_ref=fresh.at[turn], dst_ref=face_recv.at[turn, face], send_sem=fresh_ssem.at[turn, face],
+            recv_sem=face_rsem.at[turn, face], device_id=near_by[face][1], device_id_type=MESH,
+        ).wait_recv()
+
+    last = SWEEPS * COLOURS - 1
+    for turn in range(last + 1):
+        colour = turn % COLOURS
+        low = colour * colblk
+        part = slice(low, low + colblk)
+        own = state[part, :]
+        resid = load_ref[part, :] - mass_ref[part, :] * own
+        if turn > 0:
+            for face in range(4):
+                for r in range(colblk):
+                    seen[face, r:r + 1, :] = near[face, pl.ds(faces_ref[face, low + r], 1), :]
+            sides = [own] + [seen[face] for face in range(4)]
+            for k in range(chunks):
+                for h in range(cols // 128):
+                    total = None
+                    for s in range(5):
+                        at = (colour * 5 + s) * colblk
+                        term = mat[k, at:at + colblk, h * 128:(h + 1) * 128] * sides[s]
+                        total = term if total is None else total + term
+                    at = k * cols + h * 128
+                    prod[:, at:at + 128] = split(total)
+            applied = jnp.dot(prod[...], spread[...], preferred_element_type=jnp.float32)
+            resid = resid - (applied[:colblk] + applied[colblk:])
+        value = own + resid * norm[part, :]
+        state[part, :] = value
+        if turn < last:
+            fresh[turn] = value
+            for face in range(4):
+                @pl.when(near_by[face][0])
+                def _():
+                    fresh_copy(turn, face).start()
+            for face in range(4):
+                @pl.when(near_by[face][0])
+                def _():
+                    face_wait(turn, face)
+                    near[face, part, :] = face_recv[turn, face]
+    out_ref[...] = state[...]
+
+    for turn in range(last):
+        for face in range(4):
+            @pl.when(near_by[face][0])
+            def _():
+                fresh_copy(turn, face).wait_send()
+
+    def drain(k, carry):
+        far_copy(k).wait_send()
+        for d in range(pairs):
+            @pl.when(z < d)
+            def _():
+                up_copy(k, d).wait_send()
+
+            @pl.when(z > d)
+            def _():
+                down_copy(k, d).wait_send()
+        return carry
+
+    lax.fori_loop(0, chunks, drain, 0)
+
+
+def fused(tiles, owner, target, mass, rhs, faces):
+    count, width = tiles.shape[1:]
+    rowblk = mass.shape[1] // BLK
+    colblk = rowblk // COLOURS
+    peers = lax.axis_size("dev")
+    pairs = peers // 2
+    slots = rowblk * 5
+    cols = 256
+    chunks = width // cols
+    dest = owner.reshape(1, count)
+    row, side = target // 5, target % 5
+    place = ((row // colblk) * 5 + side) * colblk + row % colblk
+    key = (dest // 2) * slots + place
+    right = dest % 2
+
+    def twice(value):
+        value = value.reshape(rowblk, BLK)
+        return jnp.concatenate([value, value], axis=1)
+
+    vmem = pl.BlockSpec(memory_space=pltpu.VMEM)
+    steps = SWEEPS * COLOURS - 1
+    out = pl.pallas_call(
+        functools.partial(assemble_and_smooth, pairs, cols, (lax.axis_size("grp"), peers)),
+        out_shape=jax.ShapeDtypeStruct((rowblk, 2 * BLK), jnp.float32),
+        in_specs=[pl.BlockSpec(memory_space=pl.ANY), vmem, vmem, vmem, vmem, pl.BlockSpec(memory_space=pltpu.SMEM)],
+        out_specs=vmem,
+        scratch_shapes=[
+            pltpu.VMEM((chunks, count, cols), jnp.bfloat16),
+            pltpu.VMEM((pairs * slots, count), jnp.bfloat16),
+            pltpu.VMEM((pairs * slots, count), jnp.bfloat16),
+            pltpu.VMEM((chunks, pairs * slots, cols), jnp.bfloat16),
+            pltpu.VMEM((chunks, pairs * slots, cols), jnp.bfloat16),
+            pltpu.VMEM((4, pairs, slots, cols), jnp.float32),
+            pltpu.VMEM((chunks, pairs, slots, cols), jnp.bfloat16),
+            pltpu.VMEM((chunks, pairs, slots, cols), jnp.bfloat16),
+            pltpu.VMEM((chunks, pairs, slots, cols), jnp.bfloat16),
+            pltpu.VMEM((width, 2 * BLK), jnp.bfloat16),
+            pltpu.VMEM((chunks, slots, cols), jnp.float32),
+            pltpu.VMEM((2 * rowblk, 2 * BLK), jnp.float32),
+            pltpu.VMEM((rowblk, 2 * BLK), jnp.float32),
+            pltpu.VMEM((4, rowblk, 2 * BLK), jnp.float32),
+            pltpu.VMEM((4, colblk, 2 * BLK), jnp.float32),
+            pltpu.VMEM((2 * colblk, width), jnp.bfloat16),
+            pltpu.VMEM((steps, colblk, 2 * BLK), jnp.float32),
+            pltpu.VMEM((steps, 4, colblk, 2 * BLK), jnp.float32),
+            pltpu.SemaphoreType.DMA((chunks,)),
+            pltpu.SemaphoreType.DMA((chunks,)),
+            pltpu.SemaphoreType.DMA((chunks,)),
+            pltpu.SemaphoreType.DMA((chunks, pairs)),
+            pltpu.SemaphoreType.DMA((chunks, pairs)),
+            pltpu.SemaphoreType.DMA((chunks, pairs)),
+            pltpu.SemaphoreType.DMA((steps, 4)),
+            pltpu.SemaphoreType.DMA((steps, 4)),
+        ],
+        compiler_params=pltpu.CompilerParams(
+            collective_id=0, has_side_effects=True, vmem_limit_bytes=58 * 1024 * 1024
+        ),
+    )(tiles, key, right, twice(mass), twice(rhs), faces[:, 0, :])
+    return out[:, :BLK].reshape(1, -1)
+
 
 def solution(mesh):
     placed = (
@@ -98,6 +394,8 @@
         P("grp", "dev"),
         P(None, "grp", "dev"),
     )
+    peers = mesh.shape["dev"]
     return jax.shard_map(
-        body, mesh=mesh, in_specs=placed, out_specs=P("grp", "dev"), check_vma=False
+        fused if peers % 2 == 0 and peers <= 8 else body,
+        mesh=mesh, in_specs=placed, out_specs=P("grp", "dev"), check_vma=False,
     )

time: 655 us -> 193 us (0.29); the launches traced: 646 us -> 192 us
  waiting for transfers between devices: 371 us -> 0 us
  Pallas kernels: 0 us -> 186 us
  local copies, waits for them, and re-layouts: 107 us -> 2.05 us
  starting transfers between devices: 89.7 us -> 0 us
  other arithmetic: 43 us -> 4.81 us
  matrix products: 35.5 us -> 0 us
    all_to_all x2 -> x0, waiting for transfers between devices: 352 us -> none  [the longest x1 352 us: body(): lax.all_to_all(packed, 'dev', split_axis=0, concat_axis=0, tiled=True)]
    pallas_call x0 -> x1, Pallas kernels: none -> 186 us  [fused(): pl.pallas_call(functools.partial(assemble_and_smooth, pairs, cols, (lax.a...]
    ppermute x28 -> x0, starting transfers between devices: 78.7 us -> none  [the longest x14 60.7 us: padded(): before = lax.ppermute(last, axis, up)]
    dot_general x17 -> x0, matrix products: 35.5 us -> none  [the longest x8 12.9 us: body(): jnp.einsum('rij,rj->ri', blocks[low:upper, 0], own, precision=high)]
    gather x32 -> x0, local copies, waits for them, and re-layouts: 30.6 us -> none  [body(): jnp.take(nearby[face], links[face, low:upper], axis=0)]
    another operation x43 -> x0, other arithmetic: 29.4 us -> none  [the longest x40 27 us: body(): jnp.stack([jnp.take(nearby[face], links[face, low:upper], axis=0) for fac...]
    scatter x3 -> x0, local copies, waits for them, and re-layouts: 27 us -> none  [the longest x1 22 us: pack_slots(): jnp.zeros((peers * slots, width), jnp.bfloat16).at[place]]
    reshape x10 -> x3, local copies, waits for them, and re-layouts: 23.9 us -> 1.54 us  [the longest x1 1.39 us: fused(): return out[:, :BLK].reshape(1, -1)]
  transfers between devices with their start and end apart: 30 -> 0, of which waited for: 15 -> 0; matrix products, arithmetic and copies ran while one was open for 10% -> 0% of each run, Pallas kernels for 0% -> 0%
where the time goes in v1:
time: 193 us; the launch traced here: 192 us
  Pallas kernels  186 us (96%)
  other arithmetic  4.81 us (2%)
  local copies, waits for them, and re-layouts  2.05 us (1%)
    pallas_call x1, Pallas kernels, fused(): pl.pallas_call(functools.partial(assemble_and_smooth, pairs, cols, (lax.a...  186 us

profile of v1, /device:TPU:0, one launch (start us, length us, event | category | flops | bytes accessed | tf_op | source)
XLA Modules:
  0.0 192.4 jit_solution(16136946444473512182)
XLA Ops:
  0.0 0.5 broadcast.130
  0.5 1.4 reduce.6
  1.9 1.4 reduce.7
  3.2 0.1 reshape.158
  3.3 0.1 reshape.157
  3.4 0.7 pad_maximum_fusion
  4.1 1.4 and_select_fusion
  5.5 185.5 %shard_map.64 = f32[32,128]{1,0:T(8,128)} custom-call(bf16[1,1024,4096]{2,1,0:T(8,128)(2,1)} %tiles_hbm.1, s32[1,1024]{1,0:T(1,128)} %get-tuple-element.6.key_ref, s32[1,1024]{1,0:T(1,128)} %get-tuple-element.5.right_ref, f32[32,128]{1,0:T(8,128)} %get-tuple-element.7.mass_ref, f32[32,128]{1,0:T(8,128)} %get-tuple-element.8.load_ref, s32[4,32]{1,0:T(4,128)} %bitcast.20), custom_call_target="tpu_custom_call" | custom-call | tf_op jit(solution)/shard_map/pallas_call | solution.py:348
  191.0 1.4 reshape.159

commit v2 on v1

--- a/solution.py
+++ b/solution.py
@@ -187,7 +187,7 @@
         @pl.when(turn < chunks)
         def _():
             k = turn
-            slot = lax.rem(k, 4)
+            slot = lax.rem(k, pairs)
             far_copy(k).wait_recv()
             for d in range(pairs):
                 part = slice(d * slots, (d + 1) * slots)
@@ -205,28 +205,29 @@
                     line_send[k, d] = acc[slot, d].astype(jnp.bfloat16)
                     down_copy(k, d).start()
 
-        @pl.when((turn >= 1) & (turn < chunks + 1))
+        down_lag = pairs - 1 - z
+        for e in range(1, pairs):
+            d = pairs - e
+            @pl.when((z > 0) & (z < d) & (turn >= z) & (turn < chunks + z))
+            def _():
+                k = turn - z
+                slot = lax.rem(k, pairs)
+                up_copy(k, d).wait_recv()
+                line_send[k, d] = (acc[slot, d] + up_recv[k, d].astype(jnp.float32)).astype(jnp.bfloat16)
+                up_copy(k, d).start()
+            g = e - 1
+            @pl.when((z < pairs - 1) & (z > g) & (turn >= down_lag) & (turn < chunks + down_lag))
+            def _():
+                k = turn - down_lag
+                slot = lax.rem(k, pairs)
+                down_copy(k, g).wait_recv()
+                line_send[k, g] = (acc[slot, g] + down_recv[k, g].astype(jnp.float32)).astype(jnp.bfloat16)
+                down_copy(k, g).start()
+
+        @pl.when(turn >= pairs - 1)
         def _():
-            k = turn - 1
-            slot = lax.rem(k, 4)
-            for e in range(1, pairs):
-                d = pairs - e
-                @pl.when((z > 0) & (z < d))
-                def _():
-                    up_copy(k, d).wait_recv()
-                    line_send[k, d] = (acc[slot, d] + up_recv[k, d].astype(jnp.float32)).astype(jnp.bfloat16)
-                    up_copy(k, d).start()
-                g = e - 1
-                @pl.when((z < pairs - 1) & (z > g))
-                def _():
-                    down_copy(k, g).wait_recv()
-                    line_send[k, g] = (acc[slot, g] + down_recv[k, g].astype(jnp.float32)).astype(jnp.bfloat16)
-                    down_copy(k, g).start()
-
-        @pl.when(turn >= 2)
-        def _():
-            k = turn - 2
-            slot = lax.rem(k, 4)
+            k = turn - (pairs - 1)
+            slot = lax.rem(k, pairs)
             mat[k] = acc[slot, z]
 
             @pl.when(z > 0)
@@ -248,7 +249,7 @@
 
         return carry
 
-    lax.fori_loop(0, chunks + 2, step, 0)
+    lax.fori_loop(0, chunks + pairs - 1, step, 0)
 
     half = COLOURS * colblk
     norm[:half, :] = 1.0 / (mass_ref[...] + norm[:half, :] + norm[half:, :])
@@ -356,7 +357,7 @@
             pltpu.VMEM((pairs * slots, count), jnp.bfloat16),
             pltpu.VMEM((chunks, pairs * slots, cols), jnp.bfloat16),
             pltpu.VMEM((chunks, pairs * slots, cols), jnp.bfloat16),
-            pltpu.VMEM((4, pairs, slots, cols), jnp.float32),
+            pltpu.VMEM((pairs, pairs, slots, cols), jnp.float32),
             pltpu.VMEM((chunks, pairs, slots, cols), jnp.bfloat16),
             pltpu.VMEM((chunks, pairs, slots, cols), jnp.bfloat16),
             pltpu.VMEM((chunks, pairs, slots, cols), jnp.bfloat16),

time: 193 us -> 166 us (0.86)
  Pallas kernels: 186 us -> 159 us
    pallas_call x1, Pallas kernels: 186 us -> 159 us  [fused(): pl.pallas_call(functools.partial(assemble_and_smooth, pairs, cols, (lax.a...]
where the time goes in v2:
time: 166 us
  Pallas kernels  159 us (96%)
  other arithmetic  4.81 us (3%)
  local copies, waits for them, and re-layouts  2.05 us (1%)
    pallas_call x1, Pallas kernels, fused(): pl.pallas_call(functools.partial(assemble_and_smooth, pairs, cols, (lax.a...  159 us

profile of v2, /device:TPU:0, one launch (start us, length us, event | category | flops | bytes accessed | tf_op | source)
XLA Modules:
  0.0 165.9 jit_solution(8788667811422707136)
XLA Ops:
  0.0 0.5 broadcast.130
  0.5 1.4 reduce.6
  1.9 1.4 reduce.7
  3.2 0.1 reshape.158
  3.3 0.1 reshape.157
  3.4 0.7 pad_maximum_fusion
  4.1 1.4 and_select_fusion
  5.5 159.0 %shard_map.64 = f32[32,128]{1,0:T(8,128)} custom-call(bf16[1,1024,4096]{2,1,0:T(8,128)(2,1)} %tiles_hbm.1, s32[1,1024]{1,0:T(1,128)} %get-tuple-element.6.key_ref, s32[1,1024]{1,0:T(1,128)} %get-tuple-element.5.right_ref, f32[32,128]{1,0:T(8,128)} %get-tuple-element.7.mass_ref, f32[32,128]{1,0:T(8,128)} %get-tuple-element.8.load_ref, s32[4,32]{1,0:T(4,128)} %bitcast.20), custom_call_target="tpu_custom_call" | custom-call | tf_op jit(solution)/shard_map/pallas_call | solution.py:349
  164.5 1.4 reshape.159

commit v3 on v2

--- a/solution.py
+++ b/solution.py
@@ -93,16 +93,17 @@
                 nearby = nearby.at[:, low:upper].set(share(state[low:upper]))
     return state.reshape(1, -1)
 
-def assemble_and_smooth(pairs, cols, names, tiles_hbm, key_ref, right_ref, mass_ref, load_ref, faces_ref, out_ref,
-                        tiles_v, pick_far, pick_own, far_send, far_recv, acc, line_send, up_recv, down_recv,
+def assemble_and_smooth(pairs, cols, early, names, tiles_hbm, key_ref, right_ref, mass_ref, load_ref, faces_ref, out_ref,
+                        tiles_v, pick_far, pick_own, far_send, far_recv, acc, line_send, up_recv, down_recv, pair_send, pair_recv,
                         spread, mat, norm, state, near, seen, prod, fresh, face_recv,
-                        tile_sem, far_ssem, far_rsem, line_ssem, up_rsem, down_rsem, fresh_ssem, face_rsem):
+                        tile_sem, far_ssem, far_rsem, line_ssem, up_rsem, down_rsem, fresh_ssem, face_rsem, pair_ssem, pair_rsem):
     grp = lax.axis_index("grp")
     dev = lax.axis_index("dev")
     n_grp, n_dev = names
     z = dev // 2
     x = dev % 2
     chunks = tiles_v.shape[0]
+    lines = chunks + early
     slots = mat.shape[1]
     colblk = slots // (5 * COLOURS)
     near_by = [
@@ -144,6 +145,12 @@
             device_id={"dev": z * 2 + 1 - x}, device_id_type=MESH,
         )
 
+    def pair_copy(c):
+        return pltpu.make_async_remote_copy(
+            src_ref=pair_send.at[c], dst_ref=pair_recv.at[c], send_sem=pair_ssem.at[c], recv_sem=pair_rsem.at[c],
+            device_id={"dev": z * 2 + 1 - x}, device_id_type=MESH,
+        )
+
     def up_copy(k, d):
         return pltpu.make_async_remote_copy(
             src_ref=line_send.at[k, d], dst_ref=up_recv.at[k, d], send_sem=line_ssem.at[k, d],
@@ -166,7 +173,9 @@
         far_copy(k).start()
         return carry
 
-    lax.fori_loop(0, chunks, send_far, 0)
+    for c in range(early):
+        load_tiles(c).wait()
+    lax.fori_loop(early, chunks, send_far, 0)
 
     for d in range(pairs):
         part = slice(d * slots, (d + 1) * slots)
@@ -183,17 +192,50 @@
         top = value.astype(jnp.bfloat16).astype(jnp.float32)
         return jnp.concatenate([top, value - top], axis=0).astype(jnp.bfloat16)
 
+    def finish(v, k, slot):
+        mat[k] = acc[slot, z]
+
+        @pl.when(z > 0)
+        def _():
+            up_copy(v, z).wait_recv()
+            mat[k] = mat[k] + up_recv[v, z].astype(jnp.float32)
+
+        @pl.when(z < pairs - 1)
+        def _():
+            down_copy(v, z).wait_recv()
+            mat[k] = mat[k] + down_recv[v, z].astype(jnp.float32)
+
+    def add_norm(k):
+        size = jnp.abs(mat[k]).reshape(COLOURS, 5, colblk, cols)
+        size = jnp.sum(size, axis=1).reshape(COLOURS * colblk, cols)
+        at = k * cols if isinstance(k, int) else pl.multiple_of(k * cols, cols)
+        norm[...] += jnp.dot(split(size), spread[pl.ds(at, cols), :], preferred_element_type=jnp.float32)
+
     def step(turn, carry):
-        @pl.when(turn < chunks)
-        def _():
-            k = turn
-            slot = lax.rem(k, pairs)
+        for v in range(2 * early):
+            @pl.when(turn == v)
+            def _():
+                pick = pick_own if v % 2 else pick_far
+                for d in range(pairs):
+                    acc[v % pairs, d] = jnp.dot(
+                        pick[d * slots:(d + 1) * slots, :], tiles_v[v // 2], preferred_element_type=jnp.float32
+                    )
+
+        @pl.when((turn >= 2 * early) & (turn < lines))
+        def _():
+            k = turn - early
+            slot = lax.rem(turn, pairs)
             far_copy(k).wait_recv()
             for d in range(pairs):
                 part = slice(d * slots, (d + 1) * slots)
                 acc[slot, d] = jnp.dot(
                     pick_own[part, :], tiles_v[k], preferred_element_type=jnp.float32
                 ) + far_recv[k, part, :].astype(jnp.float32)
+
+        @pl.when(turn < lines)
+        def _():
+            k = turn
+            slot = lax.rem(k, pairs)
             for d in reversed(range(1, pairs)):
                 @pl.when(z == 0)
                 def _():
@@ -208,7 +250,7 @@
         down_lag = pairs - 1 - z
         for e in range(1, pairs):
             d = pairs - e
-            @pl.when((z > 0) & (z < d) & (turn >= z) & (turn < chunks + z))
+            @pl.when((z > 0) & (z < d) & (turn >= z) & (turn < lines + z))
             def _():
                 k = turn - z
                 slot = lax.rem(k, pairs)
@@ -216,7 +258,7 @@
                 line_send[k, d] = (acc[slot, d] + up_recv[k, d].astype(jnp.float32)).astype(jnp.bfloat16)
                 up_copy(k, d).start()
             g = e - 1
-            @pl.when((z < pairs - 1) & (z > g) & (turn >= down_lag) & (turn < chunks + down_lag))
+            @pl.when((z < pairs - 1) & (z > g) & (turn >= down_lag) & (turn < lines + down_lag))
             def _():
                 k = turn - down_lag
                 slot = lax.rem(k, pairs)
@@ -224,32 +266,28 @@
                 line_send[k, g] = (acc[slot, g] + down_recv[k, g].astype(jnp.float32)).astype(jnp.bfloat16)
                 down_copy(k, g).start()
 
-        @pl.when(turn >= pairs - 1)
-        def _():
-            k = turn - (pairs - 1)
-            slot = lax.rem(k, pairs)
-            mat[k] = acc[slot, z]
-
-            @pl.when(z > 0)
-            def _():
-                up_copy(k, z).wait_recv()
-                mat[k] = mat[k] + up_recv[k, z].astype(jnp.float32)
-
-            @pl.when(z < pairs - 1)
-            def _():
-                down_copy(k, z).wait_recv()
-                mat[k] = mat[k] + down_recv[k, z].astype(jnp.float32)
-
-            size = jnp.abs(mat[k]).reshape(COLOURS, 5, colblk, cols)
-            size = jnp.sum(size, axis=1).reshape(COLOURS * colblk, cols)
-            norm[...] += jnp.dot(
-                split(size), spread[pl.ds(pl.multiple_of(k * cols, cols), cols), :],
-                preferred_element_type=jnp.float32,
-            )
+        for v in range(2 * early):
+            @pl.when(turn == v + pairs - 1)
+            def _():
+                finish(v, v // 2, v % pairs)
+                if v % 2 == 0:
+                    pair_send[v // 2] = mat[v // 2].astype(jnp.bfloat16)
+                    pair_copy(v // 2).start()
+
+        @pl.when(turn >= 2 * early + pairs - 1)
+        def _():
+            v = turn - (pairs - 1)
+            finish(v, v - early, lax.rem(v, pairs))
+            add_norm(v - early)
 
         return carry
 
-    lax.fori_loop(0, chunks + pairs - 1, step, 0)
+    lax.fori_loop(0, lines + pairs - 1, step, 0)
+
+    for c in range(early):
+        pair_copy(c).wait_recv()
+        mat[c] = mat[c] + pair_recv[c].astype(jnp.float32)
+        add_norm(c)
 
     half = COLOURS * colblk
     norm[:half, :] = 1.0 / (mass_ref[...] + norm[:half, :] + norm[half:, :])
@@ -310,8 +348,15 @@
             def _():
                 fresh_copy(turn, face).wait_send()
 
+    def drain_far(k, carry):
+        far_copy(k).wait_send()
+        return carry
+
+    lax.fori_loop(early, chunks, drain_far, 0)
+    for c in range(early):
+        pair_copy(c).wait_send()
+
     def drain(k, carry):
-        far_copy(k).wait_send()
         for d in range(pairs):
             @pl.when(z < d)
             def _():
@@ -322,7 +367,7 @@
                 down_copy(k, d).wait_send()
         return carry
 
-    lax.fori_loop(0, chunks, drain, 0)
+    lax.fori_loop(0, lines, drain, 0)
 
 
 def fused(tiles, owner, target, mass, rhs, faces):
@@ -334,6 +379,7 @@
     slots = rowblk * 5
     cols = 256
     chunks = width // cols
+    early = chunks // 8
     dest = owner.reshape(1, count)
     row, side = target // 5, target % 5
     place = ((row // colblk) * 5 + side) * colblk + row % colblk
@@ -347,7 +393,7 @@
     vmem = pl.BlockSpec(memory_space=pltpu.VMEM)
     steps = SWEEPS * COLOURS - 1
     out = pl.pallas_call(
-        functools.partial(assemble_and_smooth, pairs, cols, (lax.axis_size("grp"), peers)),
+        functools.partial(assemble_and_smooth, pairs, cols, early, (lax.axis_size("grp"), peers)),
         out_shape=jax.ShapeDtypeStruct((rowblk, 2 * BLK), jnp.float32),
         in_specs=[pl.BlockSpec(memory_space=pl.ANY), vmem, vmem, vmem, vmem, pl.BlockSpec(memory_space=pltpu.SMEM)],
         out_specs=vmem,
@@ -358,9 +404,11 @@
             pltpu.VMEM((chunks, pairs * slots, cols), jnp.bfloat16),
             pltpu.VMEM((chunks, pairs * slots, cols), jnp.bfloat16),
             pltpu.VMEM((pairs, pairs, slots, cols), jnp.float32),
-            pltpu.VMEM((chunks, pairs, slots, cols), jnp.bfloat16),
-            pltpu.VMEM((chunks, pairs, slots, cols), jnp.bfloat16),
-            pltpu.VMEM((chunks, pairs, slots, cols), jnp.bfloat16),
+            pltpu.VMEM((chunks + early, pairs, slots, cols), jnp.bfloat16),
+            pltpu.VMEM((chunks + early, pairs, slots, cols), jnp.bfloat16),
+            pltpu.VMEM((chunks + early, pairs, slots, cols), jnp.bfloat16),
+            pltpu.VMEM((early, slots, cols), jnp.bfloat16),
+            pltpu.VMEM((early, slots, cols), jnp.bfloat16),
             pltpu.VMEM((width, 2 * BLK), jnp.bfloat16),
             pltpu.VMEM((chunks, slots, cols), jnp.float32),
             pltpu.VMEM((2 * rowblk, 2 * BLK), jnp.float32),
@@ -373,11 +421,13 @@
             pltpu.SemaphoreType.DMA((chunks,)),
             pltpu.SemaphoreType.DMA((chunks,)),
             pltpu.SemaphoreType.DMA((chunks,)),
-            pltpu.SemaphoreType.DMA((chunks, pairs)),
-            pltpu.SemaphoreType.DMA((chunks, pairs)),
-            pltpu.SemaphoreType.DMA((chunks, pairs)),
+            pltpu.SemaphoreType.DMA((chunks + early, pairs)),
+            pltpu.SemaphoreType.DMA((chunks + early, pairs)),
+            pltpu.SemaphoreType.DMA((chunks + early, pairs)),
             pltpu.SemaphoreType.DMA((steps, 4)),
             pltpu.SemaphoreType.DMA((steps, 4)),
+            pltpu.SemaphoreType.DMA((early,)),
+            pltpu.SemaphoreType.DMA((early,)),
         ],
         compiler_params=pltpu.CompilerParams(
             collective_id=0, has_side_effects=True, vmem_limit_bytes=58 * 1024 * 1024

time: 166 us -> 154 us (0.928)
  Pallas kernels: 159 us -> 146 us
    pallas_call x1, Pallas kernels: 159 us -> 146 us  [fused(): pl.pallas_call(functools.partial(assemble_and_smooth, pairs, cols, early,...]
where the time goes in v3:
time: 154 us; the launch traced here: 153 us
  Pallas kernels  146 us (95%)
  other arithmetic  4.81 us (3%)
  local copies, waits for them, and re-layouts  2.05 us (1%)
    pallas_call x1, Pallas kernels, fused(): pl.pallas_call(functools.partial(assemble_and_smooth, pairs, cols, early,...  146 us

profile of v3, /device:TPU:0, one launch (start us, length us, event | category | flops | bytes accessed | tf_op | source)
XLA Modules:
  0.0 153.0 jit_solution(5775171528028360708)
XLA Ops:
  0.0 0.5 broadcast.130
  0.5 1.4 reduce.6
  1.9 1.4 reduce.7
  3.2 0.1 reshape.158
  3.3 0.1 reshape.157
  3.4 0.7 pad_maximum_fusion
  4.1 1.4 and_select_fusion
  5.5 146.2 %shard_map.64 = f32[32,128]{1,0:T(8,128)} custom-call(bf16[1,1024,4096]{2,1,0:T(8,128)(2,1)} %tiles_hbm.1, s32[1,1024]{1,0:T(1,128)} %get-tuple-element.6.key_ref, s32[1,1024]{1,0:T(1,128)} %get-tuple-element.5.right_ref, f32[32,128]{1,0:T(8,128)} %get-tuple-element.7.mass_ref, f32[32,128]{1,0:T(8,128)} %get-tuple-element.8.load_ref, s32[4,32]{1,0:T(4,128)} %bitcast.20), custom_call_target="tpu_custom_call" | custom-call | tf_op jit(solution)/shard_map/pallas_call | solution.py:395
  151.6 1.4 reshape.159

commit v4 on v3

--- a/solution.py
+++ b/solution.py
@@ -93,10 +93,10 @@
                 nearby = nearby.at[:, low:upper].set(share(state[low:upper]))
     return state.reshape(1, -1)
 
-def assemble_and_smooth(pairs, cols, early, names, tiles_hbm, key_ref, right_ref, mass_ref, load_ref, faces_ref, out_ref,
+def assemble_and_smooth(pairs, cols, early, names, tiles_hbm, key_ref, right_ref, mass_in, load_in, faces_ref, out_ref,
                         tiles_v, pick_far, pick_own, far_send, far_recv, acc, line_send, up_recv, down_recv, pair_send, pair_recv,
                         spread, mat, norm, state, near, seen, prod, fresh, face_recv,
-                        tile_sem, far_ssem, far_rsem, line_ssem, up_rsem, down_rsem, fresh_ssem, face_rsem, pair_ssem, pair_rsem):
+                        tile_sem, far_ssem, far_rsem, line_ssem, up_rsem, down_rsem, fresh_ssem, face_rsem, pair_ssem, pair_rsem, mass_ref, load_ref):
     grp = lax.axis_index("grp")
     dev = lax.axis_index("dev")
     n_grp, n_dev = names
@@ -184,6 +184,10 @@
     unit = lax.broadcasted_iota(jnp.int32, (cols, 128), 1) % BLK
     for k in range(chunks):
         spread[k * cols:(k + 1) * cols, :] = jnp.where(lane + k * (cols // BLK) == unit, 1.0, 0.0).astype(jnp.bfloat16)
+    for r in range(mass_ref.shape[0]):
+        for flat, wide in ((mass_in, mass_ref), (load_in, load_ref)):
+            value = flat[:, r * BLK:(r + 1) * BLK]
+            wide[r:r + 1, :] = jnp.concatenate([value, value], axis=1)
     norm[...] = jnp.zeros_like(norm)
     near[...] = jnp.zeros_like(near)
     state[...] = jnp.zeros_like(state)
@@ -385,10 +389,6 @@
     place = ((row // colblk) * 5 + side) * colblk + row % colblk
     key = (dest // 2) * slots + place
     right = dest % 2
-
-    def twice(value):
-        value = value.reshape(rowblk, BLK)
-        return jnp.concatenate([value, value], axis=1)
 
     vmem = pl.BlockSpec(memory_space=pltpu.VMEM)
     steps = SWEEPS * COLOURS - 1
@@ -428,11 +428,13 @@
             pltpu.SemaphoreType.DMA((steps, 4)),
             pltpu.SemaphoreType.DMA((early,)),
             pltpu.SemaphoreType.DMA((early,)),
+            pltpu.VMEM((rowblk, 2 * BLK), jnp.float32),
+            pltpu.VMEM((rowblk, 2 * BLK), jnp.float32),
         ],
         compiler_params=pltpu.CompilerParams(
             collective_id=0, has_side_effects=True, vmem_limit_bytes=58 * 1024 * 1024
         ),
-    )(tiles, key, right, twice(mass), twice(rhs), faces[:, 0, :])
+    )(tiles, key, right, mass, rhs, faces[:, 0, :])
     return out[:, :BLK].reshape(1, -1)
 
 

time: 154 us -> 149 us (0.968)
  other arithmetic: 4.81 us -> 1.39 us
    unnamed x2 -> x0, other arithmetic: 2.73 us -> none
where the time goes in v4:
time: 149 us
  Pallas kernels  146 us (98%)
    pallas_call x1, Pallas kernels, fused(): pl.pallas_call(functools.partial(assemble_and_smooth, pairs, cols, early,...  146 us

profile of v4, /device:TPU:0, one launch (start us, length us, event | category | flops | bytes accessed | tf_op | source)
XLA Modules:
  0.0 149.0 jit_solution(7782815645111297221)
XLA Ops:
  0.0 1.4 and_select_fusion
  1.4 146.2 %shard_map.64 = f32[32,128]{1,0:T(8,128)} custom-call(bf16[1,1024,4096]{2,1,0:T(8,128)(2,1)} %tiles_hbm.1, s32[1,1024]{1,0:T(1,128)} %get-tuple-element.6.key_ref, s32[1,1024]{1,0:T(1,128)} %get-tuple-element.5.right_ref, f32[1,2048]{1,0:T(1,128)} %mass_in.1, f32[1,2048]{1,0:T(1,128)} %load_in.1, s32[4,32]{1,0:T(4,128)} %bitcast.20), custom_call_target="tpu_custom_call" | custom-call | tf_op jit(solution)/shard_map/pallas_call | solution.py:395
  147.6 1.4 reshape.151
